TPU v7x, 32 devices: a whole 2x2x4 slice. The times are simulated.
32 devices in a mesh: fam: 2 (over x), tm: 8 (over z, y), chan: 2 (over core).
Axes of the slice: x: 2, y: 2, z: 4, core: 2. Of those that a mesh axis runs over, the one named last changes fastest.
Arguments:
- records: float32 [3072, 4096], P(('fam', 'tm', 'chan')), parts along dimension 0, may hold values from -6 to 6
- row_dest: int32 [3072], P(('fam', 'tm', 'chan')), parts along dimension 0, may hold values from -1 to 7, as said below
- row_chan: int32 [3072], P(('fam', 'tm', 'chan')), parts along dimension 0, may hold values from 0 to 47, as said below
- row_len: int32 [3072], P(('fam', 'tm', 'chan')), parts along dimension 0, may hold values from 2048 to 4096
- templates: float32 [64, 16, 256], P(('fam', 'tm'), 'chan'), parts along dimension 0, may hold values from -6 to 6
- tmpl_chan: int32 [64, 16], P(('fam', 'tm'), 'chan'), parts along dimension 0, may hold values from 0 to 47
- tmpl_off: int32 [64, 16], P(('fam', 'tm'), 'chan'), parts along dimension 0, may hold values from 0 to 255
Outputs:
- detection: float32 [16, 4, 4, 3584], P(('fam', 'tm'), None, None, 'chan'), parts along dimension 0
There are 2 independent parts, one for each index of `fam`. A program takes and returns all parts, laid end to end along the dimension named above; each array names one. Nothing has to cross between parts.
Inputs may be any that keep to these rules, and one draw needn't show every extreme that they name: `row_dest`: within the slots of the owners in one channel half, every pair of a time segment and a channel appears exactly once; one owner holds at most 12 rows of one time segment, and some owner holds exactly 12 of each. `row_chan`: 0 on empty slots.
All inputs are finite; a program needn't handle non-finite values.
Results may differ from a plain program's by a relative error of at most 0.0003.
Values sent between devices are 32-bit elements; how exact they have to be, the bound alone decides.
A program may use at most 128 MiB of HBM per device.

v0:
```python
import jax
import jax.numpy as jnp
from jax import lax
from jax.sharding import PartitionSpec as P

TCH = 16
MAXOFF = 256
STOPS = 4


FLOOR_SHARE = 0.25
TEMPLATE_EPS = 1e-06
highest = lax.Precision.HIGHEST


def shifted(x, axis, by):
    devices = lax.axis_size(axis)
    return lax.ppermute(x, axis, [(i, (i + by) % devices) for i in range(devices)])


def normalized(template_rows):
    centred = template_rows - jnp.mean(template_rows, axis=-1, keepdims=True)
    energy = jnp.sum(centred * centred, axis=-1, keepdims=True)
    return centred / jnp.sqrt(energy + template_rows.shape[-1] * TEMPLATE_EPS)


def window_scale(waveform, tap_count):
    channel_count, sample_count = waveform.shape
    blocks = waveform.reshape(channel_count, sample_count // tap_count, tap_count)
    paired = jnp.concatenate([blocks[:, :-1], blocks[:, 1:]], axis=2)
    rows_idx = lax.broadcasted_iota(jnp.int32, (2 * tap_count, tap_count), 0)
    cols_idx = lax.broadcasted_iota(jnp.int32, (2 * tap_count, tap_count), 1)
    band = ((rows_idx >= cols_idx) & (rows_idx < cols_idx + tap_count)).astype(jnp.float32)
    win_sum = jnp.einsum("cbu,ur->cbr", paired, band, precision=highest).reshape(channel_count, -1)
    win_sq = jnp.einsum("cbu,ur->cbr", paired * paired, band, precision=highest).reshape(
        channel_count, -1
    )
    variance = win_sq - win_sum * win_sum / tap_count
    return 1.0 / jnp.sqrt(jnp.maximum(variance, FLOOR_SHARE * tap_count))


def toeplitz_table(pair_rows, block_width):
    pair_count, tap_count = pair_rows.shape
    window = tap_count + block_width
    padded = jnp.pad(pair_rows, ((0, 0), (0, window + 1 - tap_count)))
    tiled = jnp.tile(padded, (1, block_width))[:, : block_width * window]
    return tiled.reshape(pair_count, block_width, window)


def correlate(waveform, inv_sigma, unit_rows, chan_map, offsets):
    template_count, half_taps, tap_count = unit_rows.shape
    block_width = tap_count // 4
    shift_count = tap_count // block_width
    lag_count = waveform.shape[1] - tap_count - MAXOFF
    block_count = lag_count // block_width
    pair_rows = unit_rows.reshape(-1, tap_count)
    pair_chan = chan_map.reshape(-1)
    pair_off = offsets.reshape(-1)

    def cut_segment(channel, offset):
        return lax.dynamic_slice(waveform, (channel, offset), (1, lag_count + tap_count))[0]

    def cut_scale(channel, offset):
        return lax.dynamic_slice(inv_sigma, (channel, offset), (1, lag_count))[0]

    segments = jax.vmap(cut_segment)(pair_chan, pair_off)
    pieces = segments.reshape(segments.shape[0], -1, block_width)
    windows = jnp.concatenate(
        [pieces[:, shift : block_count + shift] for shift in range(shift_count + 1)], axis=2
    )
    toeplitz = toeplitz_table(pair_rows, block_width)
    correlation = jnp.einsum("pbu,pru->pbr", windows, toeplitz, precision=highest).reshape(
        -1, lag_count
    )
    scales = jax.vmap(cut_scale)(pair_chan, pair_off)
    ratios = (correlation * scales).reshape(template_count, half_taps, lag_count)
    stack_gain = jnp.sqrt(jnp.float32(tap_count * TCH)) / TCH
    return stack_gain * jnp.sum(ratios, axis=1)


def local(records, row_dest, row_chan, row_len, templates, tmpl_chan, tmpl_off):
    slot_count, sample_count = records.shape
    loop_size = lax.axis_size("tm")
    capacity = slot_count // loop_size
    tap_count = templates.shape[-1]
    positions = lax.broadcasted_iota(jnp.int32, records.shape, 1)
    masked = jnp.where(positions < row_len[:, None], records, jnp.zeros_like(records))
    slot_ids = jnp.arange(slot_count, dtype=jnp.int32)
    earlier = (row_dest[:, None] == row_dest[None, :]) & (slot_ids[None, :] < slot_ids[:, None])
    rank_within = jnp.sum(earlier.astype(jnp.int32), axis=1)
    target = jnp.where(row_dest >= 0, row_dest * capacity + rank_within, slot_count)
    outgoing = (
        jnp.zeros_like(masked)
        .at[target]
        .set(masked, mode="drop")
        .reshape(loop_size, capacity, sample_count)
    )
    outgoing_ids = (
        jnp.full((slot_count,), -1, jnp.int32)
        .at[target]
        .set(row_chan, mode="drop")
        .reshape(loop_size, capacity)
    )
    channel_count = slot_count // 2
    arrived, arrived_ids = (
        lax.all_to_all(outgoing, "tm", split_axis=0, concat_axis=0, tiled=True),
        lax.all_to_all(outgoing_ids, "tm", split_axis=0, concat_axis=0, tiled=True),
    )
    arrived = arrived.reshape(slot_count, sample_count)
    arrived_ids = arrived_ids.reshape(slot_count)
    places = jnp.where(arrived_ids >= 0, arrived_ids, channel_count)
    waveform = (
        jnp.zeros((channel_count, sample_count), jnp.float32).at[places].set(arrived, mode="drop")
    )
    inv_sigma = window_scale(waveform, tap_count)
    visit_start = (normalized(templates), tmpl_chan, tmpl_off)
    visiting = visit_start
    partials = []
    for stop_index in range(STOPS):
        if stop_index > 0:
            visiting = shifted((visiting[0], visiting[1], visiting[2]), "tm", 1)
        partials.append(correlate(waveform, inv_sigma, visiting[0], visiting[1], visiting[2]))
    summed = lax.psum_scatter(jnp.stack(partials), "chan", scatter_dimension=2, tiled=True)
    return summed[None]


def solution(mesh):
    in_specs = (
        P(("fam", "tm", "chan"), None),
        P(("fam", "tm", "chan")),
        P(("fam", "tm", "chan")),
        P(("fam", "tm", "chan")),
        P(("fam", "tm"), "chan", None),
        P(("fam", "tm"), "chan"),
        P(("fam", "tm"), "chan"),
    )
    out_specs = P(("fam", "tm"), None, None, "chan")
    return jax.shard_map(local, mesh=mesh, in_specs=in_specs, out_specs=out_specs, check_vma=False)
```

profile of v0, /device:TPU:0, one launch (start us, length us, event | category | flops | bytes accessed | tf_op | source)
XLA Modules:
  0.0 952.8 jit_solution(1680050459382184153)
XLA Ops:
  9.8 7.3 all-to-all-start
  30.6 4.7 all-to-all-start.1
  46.4 26.4 %collective-permute-done.3 = s32[4,8]{1,0:T(4,128)S(1)} collective-permute-done((s32[4,8]{1,0:T(4,128)S(1)}, s32[4,8]{1,0:T(4,128)S(1)}, u32[]{:S(2)}, u32[]{:S(2)}) %collective-permute-start.3) | collective-permute-done | bytes 160 | tf_op jit(solution)/shard_map/ppermute | solution.py:18
  73.2 5.9 collective-permute-done.6
  79.4 6.1 collective-permute-start.5
  116.6 62.3 %while.14 = (s32[]{:T(128)}, f32[48,4096]{1,0:T(8,128)S(1)}, s32[32,2]{0,1:T(2,128)S(1)}, f32[32,1,3840]{2,1,0:T(1,128)S(1)}, s32[]{:T(128)}) while((s32[]{:T(128)}, f32[48,4096]{1,0:T(8,128)S(1)}, s32[32,2]{0,1:T(2,128)S(1)}, f32[32,1,3840]{2,1,0:T(1,128)S(1)}, s32[]{:T(128)}) %tuple.144), condition=%wide.while_cond.6, body=%wide.while_body.6.sunk | while | flops 2 | bytes 30837 | solution.py:61
  183.6 4.9 concatenate.50
  188.5 6.4 fusion.44
  201.5 72.3 %while.15 = (s32[]{:T(128)}, f32[48,3840]{1,0:T(8,128)S(1)}, s32[32,2]{0,1:T(2,128)S(1)}, f32[32,1,3584]{2,0,1:T(8,128)S(1)}, s32[]{:T(128)}, /*index=5*/s32[]{:T(128)}) while((s32[]{:T(128)}, f32[48,3840]{1,0:T(8,128)S(1)}, s32[32,2]{0,1:T(2,128)S(1)}, f32[32,1,3584]{2,0,1:T(8,128)S(1)}, s32[]{:T(128)}, /*index=5*/s32[]{:T(128)}) %tuple.173), condition=%wide.while_cond.7, body=%wide.while_body.7.sunk | while | flops 2 | bytes 57469 | solution.py:64
  275.7 92.8 %while.12 = (s32[]{:T(128)}, f32[48,4096]{1,0:T(8,128)}, s32[32,2]{0,1:T(2,128)S(1)}, f32[32,1,3840]{2,1,0:T(1,128)S(1)}, s32[]{:T(128)}) while((s32[]{:T(128)}, f32[48,4096]{1,0:T(8,128)}, s32[32,2]{0,1:T(2,128)S(1)}, f32[32,1,3840]{2,1,0:T(1,128)S(1)}, s32[]{:T(128)}) %tuple.170), condition=%wide.while_cond.4, body=%wide.while_body.4.sunk | while | flops 2 | bytes 30837 | solution.py:61
  372.3 4.9 concatenate.47
  377.2 6.3 fusion.43
  385.8 103.7 %while.13 = (s32[]{:T(128)}, f32[48,3840]{1,0:T(8,128)}, s32[32,2]{0,1:T(2,128)S(1)}, f32[32,1,3584]{2,0,1:T(8,128)S(1)}, s32[]{:T(128)}, /*index=5*/s32[]{:T(128)}) while((s32[]{:T(128)}, f32[48,3840]{1,0:T(8,128)}, s32[32,2]{0,1:T(2,128)S(1)}, f32[32,1,3584]{2,0,1:T(8,128)S(1)}, s32[]{:T(128)}, /*index=5*/s32[]{:T(128)}) %tuple.174), condition=%wide.while_cond.5, body=%wide.while_body.5.sunk | while | flops 2 | bytes 57469 | solution.py:64
  490.6 93.7 %while.10 = (s32[]{:T(128)}, f32[48,4096]{1,0:T(8,128)}, s32[32,2]{0,1:T(2,128)S(1)}, f32[32,1,3840]{2,1,0:T(1,128)S(1)}, s32[]{:T(128)}) while((s32[]{:T(128)}, f32[48,4096]{1,0:T(8,128)}, s32[32,2]{0,1:T(2,128)S(1)}, f32[32,1,3840]{2,1,0:T(1,128)S(1)}, s32[]{:T(128)}) %tuple.171), condition=%wide.while_cond.2, body=%wide.while_body.2.sunk | while | flops 2 | bytes 30837 | solution.py:61
  588.2 5.1 concatenate.44
  593.3 6.4 fusion.42
  601.9 101.6 %while.11 = (s32[]{:T(128)}, f32[48,3840]{1,0:T(8,128)}, s32[32,2]{0,1:T(2,128)S(1)}, f32[32,1,3584]{2,0,1:T(8,128)S(1)}, s32[]{:T(128)}, /*index=5*/s32[]{:T(128)}) while((s32[]{:T(128)}, f32[48,3840]{1,0:T(8,128)}, s32[32,2]{0,1:T(2,128)S(1)}, f32[32,1,3584]{2,0,1:T(8,128)S(1)}, s32[]{:T(128)}, /*index=5*/s32[]{:T(128)}) %tuple.175), condition=%wide.while_cond.3, body=%wide.while_body.3.sunk | while | flops 2 | bytes 57469 | solution.py:64
  704.5 90.6 %while.8 = (s32[]{:T(128)}, f32[48,4096]{1,0:T(8,128)}, s32[32,2]{0,1:T(2,128)S(1)}, f32[32,1,3840]{2,1,0:T(1,128)S(1)}, s32[]{:T(128)}) while((s32[]{:T(128)}, f32[48,4096]{1,0:T(8,128)}, s32[32,2]{0,1:T(2,128)S(1)}, f32[32,1,3840]{2,1,0:T(1,128)S(1)}, s32[]{:T(128)}) %tuple.172), condition=%wide.while_cond, body=%wide.while_body.sunk | while | flops 2 | bytes 30837 | solution.py:61
  799.0 4.9 concatenate.40
  803.9 6.4 fusion.41
  812.7 101.6 %while.9 = (s32[]{:T(128)}, f32[48,3840]{1,0:T(8,128)}, s32[32,2]{0,1:T(2,128)S(1)}, f32[32,1,3584]{2,0,1:T(8,128)S(1)}, s32[]{:T(128)}, /*index=5*/s32[]{:T(128)}) while((s32[]{:T(128)}, f32[48,3840]{1,0:T(8,128)}, s32[32,2]{0,1:T(2,128)S(1)}, f32[32,1,3584]{2,0,1:T(8,128)S(1)}, s32[]{:T(128)}, /*index=5*/s32[]{:T(128)}) %tuple.176), condition=%wide.while_cond.1, body=%wide.while_body.1.sunk | while | flops 2 | bytes 57469 | solution.py:64
  915.6 5.0 copy.19
  920.5 6.7 reshape.706
  927.3 10.6 %reduce-scatter.4.cloned.1.call-done = f32[1792,16]{1,0:T(8,128)} async-done(((f32[3584,16]{1,0:T(8,128)}), f32[1792,16]{1,0:T(8,128)}) %reduce-scatter.4.cloned.1.call-update) | async-done | bytes 114704
  (1052 shorter events, 813.7 us)
Async XLA Ops:
  9.8 20.8 %all-to-all-start = ((s32[8,1,12]{2,1,0:T(1,128)}), s32[8,1,12]{2,1,0:T(1,128)S(1)}, u32[]{:S(2)}, u32[]{:S(2)}) async-start(s32[8,1,12]{2,1,0:T(1,128)} %bitcast), calls=%async_computation | async-start | bytes 8192 | tf_op jit(solution)/shard_map/all_to_all | solution.py:107
  17.1 25.7 %collective-permute-start = (s32[4,8]{1,0:T(4,128)}, s32[4,8]{1,0:T(4,128)S(1)}, u32[]{:S(2)}, u32[]{:S(2)}) collective-permute-start(s32[4,8]{1,0:T(4,128)} %param.12), channel_id=1, source_target_pairs={{0,2},{2,4},{4,6},{6,8},{8,10},{10,12},{12,14},{14,0},{1,3},{3,5},... | collective-permute-start | bytes 392 | tf_op jit(solution)/shard_map/ppermute | solution.py:18
  19.1 25.7 %collective-permute-start.1 = (s32[4,8]{1,0:T(4,128)}, s32[4,8]{1,0:T(4,128)S(1)}, u32[]{:S(2)}, u32[]{:S(2)}) collective-permute-start(s32[4,8]{1,0:T(4,128)} %param.13), channel_id=1, source_target_pairs={{0,2},{2,4},{4,6},{6,8},{8,10},{10,12},{12,14},{14,0},{1,3},{3,5},... | collective-permute-start | bytes 392 | tf_op jit(solution)/shard_map/ppermute | solution.py:18
  23.2 56.3 %collective-permute-start.2 = (f32[4,8,256]{2,1,0:T(8,128)S(1)}, f32[4,8,256]{2,1,0:T(8,128)S(1)}, u32[]{:S(2)}, u32[]{:S(2)}) collective-permute-start(f32[4,8,256]{2,1,0:T(8,128)S(1)} %subtract_divide_fusion), channel_id=1, source_target_pairs={{0,2},{2,4},{4,6},{6,8},{8,10},{10,12},{12,14},{14,0},{1,3},{3,5},... | collective-permute-start | bytes 98312 | tf_op jit(solution)/shard_map/ppermute | solution.py:18
  30.6 4.7 copy-start.16
  30.6 82.1 %all-to-all-start.1 = ((f32[8,12,4096]{2,1,0:T(8,128)}), f32[8,12,4096]{2,1,0:T(8,128)}, u32[]{:S(2)}, u32[]{:S(2)}) async-start(f32[8,12,4096]{2,1,0:T(8,128)} %reshape.503), calls=%async_computation.1 | async-start | bytes 4194304 | tf_op jit(solution)/shard_map/all_to_all | solution.py:106
  35.3 902.5 %reduce-scatter.4.cloned.1.call-start = ((), (), s32[]{:S(2)}) async-start(), calls=%async_computation.3 | async-start | bytes 2752512
  38.4 1.7 slice-start
  42.7 30.1 %collective-permute-start.3 = (s32[4,8]{1,0:T(4,128)S(1)}, s32[4,8]{1,0:T(4,128)S(1)}, u32[]{:S(2)}, u32[]{:S(2)}) collective-permute-start(s32[4,8]{1,0:T(4,128)S(1)} %collective-permute-done), channel_id=1, source_target_pairs={{0,2},{2,4},{4,6},{6,8},{8,10},{10,12},{12,14},{14,0},{1,3},{3,5},... | collective-permute-start | bytes 392 | tf_op jit(solution)/shard_map/ppermute | solution.py:18
  44.9 28.0 %collective-permute-start.4 = (s32[4,8]{1,0:T(4,128)S(1)}, s32[4,8]{1,0:T(4,128)S(1)}, u32[]{:S(2)}, u32[]{:S(2)}) collective-permute-start(s32[4,8]{1,0:T(4,128)S(1)} %collective-permute-done.1), channel_id=1, source_target_pairs={{0,2},{2,4},{4,6},{6,8},{8,10},{10,12},{12,14},{14,0},{1,3},{3,5},... | collective-permute-start | bytes 392 | tf_op jit(solution)/shard_map/ppermute | solution.py:18
  72.8 6.4 collective-permute-start.6
  73.0 6.3 collective-permute-start.7
  79.4 7.7 collective-permute-start.5
  87.1 18.3 %collective-permute-start.8 = (f32[4,8,256]{2,1,0:T(8,128)S(1)}, f32[4,8,256]{2,1,0:T(8,128)S(1)}, u32[]{:S(2)}, u32[]{:S(2)}) collective-permute-start(f32[4,8,256]{2,1,0:T(8,128)S(1)} %collective-permute-done.5), channel_id=1, source_target_pairs={{0,2},{2,4},{4,6},{6,8},{8,10},{10,12},{12,14},{14,0},{1,3},{3,5},... | collective-permute-start | bytes 98312 | tf_op jit(solution)/shard_map/ppermute | solution.py:18
  183.6 4.9 copy-start.3
  372.3 4.9 copy-start.2
  588.2 5.2 copy-start.1
  799.0 4.9 copy-start
  810.3 104.0 %copy-start.6 = (f32[32,1,3584]{2,0,1:T(8,128)S(1)}, f32[32,1,3584]{2,0,1:T(8,128)}, u32[]{:S(2)}) copy-start(f32[32,1,3584]{2,0,1:T(8,128)} %copy-done.5) | copy-start | bytes 1376260
  810.3 104.0 %copy-start.11 = (f32[4,8,3584]{2,1,0:T(8,128)S(1)}, f32[4,8,3584]{2,1,0:T(8,128)}, u32[]{:S(2)}) copy-start(f32[4,8,3584]{2,1,0:T(8,128)} %reshape.525) | copy-start | bytes 1376260
  810.3 104.2 %copy-start.8 = (f32[32,1,3584]{2,0,1:T(8,128)S(1)}, f32[32,1,3584]{2,0,1:T(8,128)}, u32[]{:S(2)}) copy-start(f32[32,1,3584]{2,0,1:T(8,128)} %copy-done.7) | copy-start | bytes 1376260
  810.3 104.2 %copy-start.12 = (f32[4,8,3584]{2,1,0:T(8,128)S(1)}, f32[4,8,3584]{2,1,0:T(8,128)}, u32[]{:S(2)}) copy-start(f32[4,8,3584]{2,1,0:T(8,128)} %reshape.520) | copy-start | bytes 1376260
  810.3 104.4 %copy-start.10 = (f32[32,1,3584]{2,0,1:T(8,128)S(1)}, f32[32,1,3584]{2,0,1:T(8,128)}, u32[]{:S(2)}) copy-start(f32[32,1,3584]{2,0,1:T(8,128)} %copy-done.9) | copy-start | bytes 1376260
  810.3 104.4 %copy-start.13 = (f32[4,8,3584]{2,1,0:T(8,128)S(1)}, f32[4,8,3584]{2,1,0:T(8,128)}, u32[]{:S(2)}) copy-start(f32[4,8,3584]{2,1,0:T(8,128)} %reshape.515) | copy-start | bytes 1376260
  (9 other events, 10.3 us)
Sparse Core Ops, SparseCore 0:
  927.4 10.4 reduce-scatter.3
where the time goes:
time: 967 us; the launch traced here: 953 us
  local copies, waits for them, and re-layouts  817 us (84%)
  waiting for transfers between devices  43.3 us (4%)
  starting transfers between devices  30.3 us (3%)
  matrix products  27.3 us (3%)
  between operations  14.1 us (1%)
  other arithmetic  13.3 us (1%)
    gather x896, local copies, waits for them, and re-layouts  712 us
    ppermute x9, waiting for transfers between devices, shifted(): lax.ppermute(x, axis, [(i, (i + by) % devices) for i in range(devices)])  32.7 us
    unnamed x48, local copies, waits for them, and re-layouts  27.1 us
    dot_general x4, matrix products, correlate(): jnp.einsum('pbu,pru->pbr', windows, toeplitz, precision=highest)  25.4 us
    concatenate x4, local copies, waits for them, and re-layouts, correlate(): jnp.concatenate([pieces[:, shift:block_count + shift] for shift in range(...  19.9 us
  transfers between devices with their start and end apart: 12, of which 5 were waited for; matrix products, arithmetic and copies ran while one was open for 3% of the time, Pallas kernels for 0%

commit v1 on v0

v1 whole, which is shorter than its diff:
```python
import functools
import math

import jax
import jax.numpy as jnp
from jax import lax
from jax.experimental import pallas as pl
from jax.experimental.pallas import tpu as pltpu
from jax.sharding import PartitionSpec as P

MAXOFF = 256
STOPS = 4
FLOOR_SHARE = 0.25
TEMPLATE_EPS = 1e-06
LANES = 128


def flat_shift(x, by):
    rows = x.shape[-2]
    if by == LANES:
        return pltpu.roll(x, rows - 1, x.ndim - 2)
    lane = lax.broadcasted_iota(jnp.int32, x.shape, x.ndim - 1)
    moved = pltpu.roll(x, LANES - by, x.ndim - 1)
    below = pltpu.roll(moved, rows - 1, x.ndim - 2)
    return jnp.where(lane < LANES - by, moved, below)


def window_total(x, taps):
    span = 1
    while span < taps:
        x = x + flat_shift(x, span)
        span *= 2
    return x


def split(x):
    hi = x.astype(jnp.bfloat16)
    lo = (x - hi.astype(jnp.float32)).astype(jnp.bfloat16)
    return hi, lo


def correlate_kernel(
    gain, half_taps, chan_slot, pair_chan, pair_off, rows_ref, tmpl_ref, out_ref, unit_ref, win_ref, scale_ref
):
    pair_count, taps = tmpl_ref.shape
    channel_count = scale_ref.shape[0]
    blocks = rows_ref.shape[1]
    out_blocks = out_ref.shape[1]

    raw = tmpl_ref[...]
    centred = raw - jnp.mean(raw, axis=-1, keepdims=True)
    energy = jnp.sum(centred * centred, axis=-1, keepdims=True)
    unit_ref[...] = centred / jnp.sqrt(energy + taps * TEMPLATE_EPS)

    def one_channel(channel):
        x = rows_ref[chan_slot[channel]]
        win_sum = window_total(x, taps)
        win_sq = window_total(x * x, taps)
        variance = win_sq - win_sum * win_sum / taps
        scale_ref[channel] = gain / jnp.sqrt(jnp.maximum(variance, FLOOR_SHARE * taps))
        hi, lo = split(jnp.concatenate([x, pltpu.roll(x, blocks - 1, 0)], axis=1))
        win_ref[channel, :blocks] = hi
        win_ref[channel, blocks:] = lo

    def channel_group(group, carry):
        for j in range(4):
            one_channel(group * 4 + j)
        return carry

    lax.fori_loop(0, channel_count // 4, channel_group, 0)

    u_pos = lax.broadcasted_iota(jnp.int32, (LANES, LANES), 0)
    r_pos = lax.broadcasted_iota(jnp.int32, (LANES, LANES), 1)
    lower = u_pos >= r_pos
    lane = lax.broadcasted_iota(jnp.int32, (blocks, LANES), 1)
    none = jnp.zeros((LANES, LANES), jnp.bfloat16)

    def toeplitz(part):
        around, full = part[:, :LANES], part[:, LANES:]
        zero = jnp.zeros_like(around)
        top = jnp.concatenate([jnp.where(lower, around, zero).astype(jnp.bfloat16), none], axis=1)
        bottom = jnp.concatenate(
            [full.astype(jnp.bfloat16), jnp.where(lower, zero, around).astype(jnp.bfloat16)], axis=1
        )
        return jnp.concatenate([top, bottom], axis=0)

    def one_pair(pair):
        row = jnp.broadcast_to(unit_ref[pl.ds(pair, 1), :], (LANES, taps))
        table = pltpu.roll(row, 0, 1, stride=1, stride_axis=0)
        hi = table.astype(jnp.bfloat16).astype(jnp.float32)
        lo = table - hi
        channel = pair_chan[pair]
        windows = win_ref[channel]
        first = jnp.dot(windows, toeplitz(hi), preferred_element_type=jnp.float32)
        second = jnp.dot(windows[:blocks], toeplitz(lo), preferred_element_type=jnp.float32)
        both = first[:blocks] + first[blocks:] + second
        corr = both[:, :LANES] + pltpu.roll(both[:, LANES:], blocks - 1, 0)
        ratio = corr * scale_ref[channel]
        offset = pair_off[pair]
        low = lax.rem(offset, LANES)
        high = offset // LANES
        moved = pltpu.roll(ratio, lax.rem(LANES - low, LANES), 1)
        below = pltpu.roll(moved, blocks - 1, 0)
        below2 = pltpu.roll(moved, blocks - 2, 0)
        far = high > 0
        return jnp.where(lane < LANES - low, jnp.where(far, below, moved), jnp.where(far, below2, below))

    def one_template(template, carry):
        total = one_pair(template * half_taps)
        for i in range(1, half_taps):
            total = total + one_pair(template * half_taps + i)
        out_ref[template] = total[:out_blocks]
        return carry

    lax.fori_loop(0, out_ref.shape[0], one_template, 0)


def local(records, row_dest, row_chan, row_len, templates, tmpl_chan, tmpl_off):
    slot_count, sample_count = records.shape
    loop_size = lax.axis_size("tm")
    half_count = lax.axis_size("chan")
    capacity = slot_count // loop_size
    template_count, half_taps, tap_count = templates.shape
    assert tap_count == 2 * LANES
    blocks = sample_count // LANES
    lag_count = sample_count - tap_count - MAXOFF
    out_blocks = lag_count // LANES
    channel_count = slot_count // 2

    positions = lax.broadcasted_iota(jnp.int32, records.shape, 1)
    masked = jnp.where(positions < row_len[:, None], records, jnp.zeros_like(records))
    masked = masked.reshape(slot_count, blocks, LANES)
    slot_ids = jnp.arange(slot_count, dtype=jnp.int32)
    earlier = (row_dest[:, None] == row_dest[None, :]) & (slot_ids[None, :] < slot_ids[:, None])
    rank_within = jnp.sum(earlier.astype(jnp.int32), axis=1)
    target = jnp.where(row_dest >= 0, row_dest * capacity + rank_within, slot_count)
    outgoing = jnp.zeros_like(masked).at[target].set(masked, mode="drop")
    outgoing_ids = jnp.sum(
        jnp.where(target[None, :] == slot_ids[:, None], row_chan[None, :] + 1, 0), axis=1
    ) - 1
    arrived = lax.all_to_all(outgoing, "tm", split_axis=0, concat_axis=0, tiled=True)
    arrived_ids = lax.all_to_all(outgoing_ids, "tm", split_axis=0, concat_axis=0, tiled=True)

    extra = jnp.stack([tmpl_chan.reshape(-1), tmpl_off.reshape(-1)], axis=1).astype(jnp.float32)
    block = jnp.concatenate(
        [templates.reshape(-1, tap_count), jnp.pad(extra, ((0, 0), (0, LANES - 2)))], axis=1
    )
    visits = [block] + [
        lax.ppermute(block, "tm", [(i, (i + by) % loop_size) for i in range(loop_size)])
        for by in range(1, STOPS)
    ]
    visits = jnp.concatenate(visits, axis=0)
    taps_back = jnp.roll(visits[:, :tap_count][:, ::-1], 1, axis=1)
    pair_chan = visits[:, tap_count].astype(jnp.int32)
    pair_off = visits[:, tap_count + 1].astype(jnp.int32)
    channels = jnp.arange(channel_count, dtype=jnp.int32)
    chan_slot = jnp.sum(
        jnp.where(arrived_ids[None, :] == channels[:, None], slot_ids[None, :], 0), axis=1
    )

    pair_count = visits.shape[0]
    gain = math.sqrt(tap_count * half_taps * half_count) / (half_taps * half_count)
    smem = pl.BlockSpec(memory_space=pltpu.SMEM)
    vmem = pl.BlockSpec(memory_space=pltpu.VMEM)
    partial = pl.pallas_call(
        functools.partial(correlate_kernel, gain, half_taps),
        out_shape=jax.ShapeDtypeStruct((STOPS * template_count, out_blocks, LANES), jnp.float32),
        in_specs=[smem, smem, smem, vmem, vmem],
        out_specs=vmem,
        scratch_shapes=[
            pltpu.VMEM((pair_count, tap_count), jnp.float32),
            pltpu.VMEM((channel_count, 2 * blocks, tap_count), jnp.bfloat16),
            pltpu.VMEM((channel_count, blocks, LANES), jnp.float32),
        ],
        compiler_params=pltpu.CompilerParams(vmem_limit_bytes=40 * 2**20),
        cost_estimate=pl.CostEstimate(
            flops=2 * 3 * pair_count * blocks * tap_count * tap_count,
            bytes_accessed=8 * slot_count * sample_count,
            transcendentals=0,
        ),
    )(chan_slot, pair_chan, pair_off, arrived, taps_back)

    half = lax.axis_index("chan")
    share = out_blocks // half_count
    keep = lax.dynamic_slice_in_dim(partial, half * share, share, 1)
    send = lax.dynamic_slice_in_dim(partial, (1 - half) * share, share, 1)
    got = lax.ppermute(send, "chan", [(0, 1), (1, 0)])
    return (keep + got).reshape(1, STOPS, template_count, share * LANES)


def solution(mesh):
    in_specs = (
        P(("fam", "tm", "chan"), None),
        P(("fam", "tm", "chan")),
        P(("fam", "tm", "chan")),
        P(("fam", "tm", "chan")),
        P(("fam", "tm"), "chan", None),
        P(("fam", "tm"), "chan"),
        P(("fam", "tm"), "chan"),
    )
    out_specs = P(("fam", "tm"), None, None, "chan")
    return jax.shard_map(local, mesh=mesh, in_specs=in_specs, out_specs=out_specs, check_vma=False)
```

time: 967 us -> 95.1 us (0.10); the launches traced: 953 us -> 93.8 us
  local copies, waits for them, and re-layouts: 817 us -> 17.3 us
  matrix products: 27.3 us -> 0 us
  Pallas kernels: 0 us -> 18.1 us
  between operations: 14.1 us -> 0.14 us
  starting transfers between devices: 30.3 us -> 19.5 us
    gather x896 -> x0, local copies, waits for them, and re-layouts: 712 us -> none
    dot_general x6 -> x0, matrix products: 27.3 us -> none  [the longest x4 25.4 us: correlate(): jnp.einsum('pbu,pru->pbr', windows, toeplitz, precision=highest)]
    unnamed x48 -> x9, local copies, waits for them, and re-layouts: 27.1 us -> 0.58 us
    reshape x19 -> x1, local copies, waits for them, and re-layouts: 24.8 us -> 0.69 us  [local(): return (keep + got).reshape(1, STOPS, template_count, share * LANES)]
    concatenate x5 -> x0, local copies, waits for them, and re-layouts: 20.3 us -> none  [the longest x4 19.9 us: correlate(): jnp.concatenate([pieces[:, shift:block_count + shift] for shift in range(...]
    pallas_call x0 -> x1, Pallas kernels: none -> 18.1 us  [local(): pl.pallas_call(functools.partial(correlate_kernel, gain, half_taps), out_...]
    slice x13 -> x2, local copies, waits for them, and re-layouts: 16 us -> 0.1 us  [local(): taps_back = jnp.roll(visits[:, :tap_count][:, ::-1], 1, axis=1)]
    ppermute x9 -> x4, starting transfers between devices: 18.3 us -> 5.97 us  [the longest x3 5.9 us: local(): lax.ppermute(block, 'tm', [(i, (i + by) % loop_size) for i in range(loop_...]
  transfers between devices with their start and end apart: 12 -> 6, of which waited for: 5 -> 3; matrix products, arithmetic and copies ran while one was open for 3% -> 20% of each run, Pallas kernels for 0% -> 0%
where the time goes in v1:
time: 95.1 us; the launch traced here: 93.8 us
  waiting for transfers between devices  34.3 us (36%)
  starting transfers between devices  19.5 us (21%)
  Pallas kernels  18.1 us (19%)
  local copies, waits for them, and re-layouts  17.3 us (18%)
  other arithmetic  4.42 us (5%)
    ppermute x3, waiting for transfers between devices, local(): lax.ppermute(block, 'tm', [(i, (i + by) % loop_size) for i in range(loop_...  33 us
    pallas_call x1, Pallas kernels, local(): pl.pallas_call(functools.partial(correlate_kernel, gain, half_taps), out_...  18.1 us
    scatter x1, local copies, waits for them, and re-layouts, local(): outgoing = jnp.zeros_like(masked).at[target].set(masked, mode='drop')  13 us
    all_to_all x1, starting transfers between devices, local(): lax.all_to_all(outgoing_ids, 'tm', split_axis=0, concat_axis=0, tiled=True)  7.28 us
    all_to_all x1, starting transfers between devices, local(): lax.all_to_all(outgoing, 'tm', split_axis=0, concat_axis=0, tiled=True)  6.29 us
    ppermute x3, starting transfers between devices, local(): lax.ppermute(block, 'tm', [(i, (i + by) % loop_size) for i in range(loop_...  5.9 us
  transfers between devices with their start and end apart: 6, of which 3 were waited for; matrix products, arithmetic and copies ran while one was open for 20% of the time, Pallas kernels for 0%

profile of v1, /device:TPU:0, one launch (start us, length us, event | category | flops | bytes accessed | tf_op | source)
XLA Modules:
  0.0 93.8 jit_solution(15897812206238187573)
XLA Ops:
  0.0 0.9 convert_reduce_fusion
  0.9 0.7 compare_select_fusion
  1.7 0.7 sub.10
  2.4 7.3 %all-to-all-start = ((s32[8,12,1]{1,2,0:T(1,128)}), s32[8,12,1]{1,2,0:T(1,128)S(1)}, u32[]{:S(2)}, u32[]{:S(2)}) async-start(s32[8,12,1]{1,2,0:T(1,128)} %bitcast), calls=%async_computation | async-start | bytes 8192 | tf_op jit(solution)/shard_map/all_to_all | solution.py:142
  9.7 1.6 %select_bitcast_fusion = f32[12,8,32,128]{3,1,2,0:T(8,128)S(1)} fusion(f32[96,4096]{1,0:T(8,128)} %param.7, s32[96]{0:T(128)} %param.10), kind=kLoop, calls=%fused_computation.1 | loop fusion | flops 786432 | bytes 3146112
  11.3 0.3 copy.18
  11.6 1.4 %broadcast_in_dim.53 = f32[96,32,128]{2,1,0:T(8,128)} broadcast(f32[]{:T(128)} %constant.3.clone.1), dimensions={} | broadcast | bytes 1572868 | tf_op jit(solution)/shard_map/broadcast_in_dim | solution.py:137
  12.9 13.0 %scatter_fusion = f32[96,32,128]{2,1,0:T(8,128)} fusion(f32[96,32,128]{2,1,0:T(8,128)} %broadcast_in_dim.53, s32[96]{0:T(128)S(1)} %get-tuple-element.7, f32[96,32,128]{2,1,0:T(8,128)S(1)} %bitcast.7), kind=kCustom, calls=%fused_computation | custom fusion | bytes 4718976 | tf_op jit(solution)/shard_map/scatter | solution.py:137
  25.9 6.3 %all-to-all-start.1 = ((f32[96,32,128]{2,1,0:T(8,128)}), f32[96,32,128]{2,1,0:T(8,128)S(1)}, u32[]{:S(2)}, u32[]{:S(2)}) async-start(f32[96,32,128]{2,1,0:T(8,128)} %scatter_fusion), calls=%async_computation.1 | async-start | bytes 3145728 | tf_op jit(solution)/shard_map/all_to_all | solution.py:141
  32.5 2.1 %collective-permute-start = (f32[32,384]{1,0:T(8,128)S(1)}, f32[32,384]{1,0:T(8,128)S(1)}, u32[]{:S(2)}, u32[]{:S(2)}) collective-permute-start(f32[32,384]{1,0:T(8,128)S(1)} %pad_maximum_fusion.2), channel_id=1, source_target_pairs={{0,2},{2,4},{4,6},{6,8},{8,10},{10,12},{12,14},{14,0},{1,3},{3,5},... | collective-permute-start | bytes 147464 | tf_op jit(solution)/shard_map/ppermute | solution.py:149
  34.6 1.5 %collective-permute-start.1 = (f32[32,384]{1,0:T(8,128)S(1)}, f32[32,384]{1,0:T(8,128)S(1)}, u32[]{:S(2)}, u32[]{:S(2)}) collective-permute-start(f32[32,384]{1,0:T(8,128)S(1)} %pad_maximum_fusion.2), channel_id=1, source_target_pairs={{0,4},{2,6},{4,8},{6,10},{8,12},{10,14},{12,0},{14,2},{1,5},{3,7},... | collective-permute-start | bytes 147464 | tf_op jit(solution)/shard_map/ppermute | solution.py:149
  36.0 2.4 %collective-permute-start.2 = (f32[32,384]{1,0:T(8,128)S(1)}, f32[32,384]{1,0:T(8,128)S(1)}, u32[]{:S(2)}, u32[]{:S(2)}) collective-permute-start(f32[32,384]{1,0:T(8,128)S(1)} %pad_maximum_fusion.2), channel_id=1, source_target_pairs={{0,6},{2,8},{4,10},{6,12},{8,14},{10,0},{12,2},{14,4},{1,7},{3,9},... | collective-permute-start | bytes 147464 | tf_op jit(solution)/shard_map/ppermute | solution.py:149
  38.4 0.5 broadcast.33
  38.9 0.7 reduce.7
  39.7 0.1 select_reduce_fusion.1.chan_slot
  39.8 23.5 %collective-permute-done = f32[32,384]{1,0:T(8,128)S(1)} collective-permute-done((f32[32,384]{1,0:T(8,128)S(1)}, f32[32,384]{1,0:T(8,128)S(1)}, u32[]{:S(2)}, u32[]{:S(2)}) %collective-permute-start) | collective-permute-done | bytes 49184 | tf_op jit(solution)/shard_map/ppermute | solution.py:149
  63.3 9.5 %collective-permute-done.2 = f32[32,384]{1,0:T(8,128)S(1)} collective-permute-done((f32[32,384]{1,0:T(8,128)S(1)}, f32[32,384]{1,0:T(8,128)S(1)}, u32[]{:S(2)}, u32[]{:S(2)}) %collective-permute-start.2) | collective-permute-done | bytes 49184 | tf_op jit(solution)/shard_map/ppermute | solution.py:149
  72.9 0.2 reverse.2
  73.1 0.1 slice.36
  73.2 0.2 fusion
  73.4 0.1 pad_maximum_fusion.1.tmpl_ref
  73.5 18.1 %shard_map.73 = f32[16,28,128]{2,1,0:T(8,128)S(1)} custom-call(s32[48]{0:T(128)S(1)} %select_reduce_fusion.1.chan_slot, s32[128]{0:T(128)S(1)} %get-tuple-element.6.pair_chan, s32[128]{0:T(128)S(1)} %get-tuple-element.5.pair_off, f32[96,32,128]{2,1,0:T(8,128)S(1)} %all-to-all-done.1.rows_ref, f32[128,256]{1,0:T(8,128)S(1)} %pad_maximum_fusion.1.tmpl_ref), custom_call_target="tpu_custom_call" | custom-call | flops 1610612736 | bytes 3145728 | tf_op jit(solution)/shard_map/pallas_call | solution.py:165
  91.7 1.3 %collective-permute-done.3 = f32[16,14,128]{2,1,0:T(8,128)S(1)} collective-permute-done((f32[16,14,128]{2,1,0:T(8,128)S(1)}, f32[16,14,128]{2,1,0:T(8,128)S(1)}, u32[]{:S(2)}, u32[]{:S(2)}) %collective-permute-start.3) | collective-permute-done | bytes 114720 | tf_op jit(solution)/shard_map/ppermute | solution.py:187
  93.1 0.7 reshape.35
  (24 shorter events, 0.7 us)
Async XLA Ops:
  2.4 23.5 %all-to-all-start = ((s32[8,12,1]{1,2,0:T(1,128)}), s32[8,12,1]{1,2,0:T(1,128)S(1)}, u32[]{:S(2)}, u32[]{:S(2)}) async-start(s32[8,12,1]{1,2,0:T(1,128)} %bitcast), calls=%async_computation | async-start | bytes 8192 | tf_op jit(solution)/shard_map/all_to_all | solution.py:142
  25.9 6.3 %copy-start.1 = (s32[4,8]{1,0:T(4,128)S(1)}, s32[4,8]{1,0:T(4,128)}, u32[]{:S(2)}) copy-start(s32[4,8]{1,0:T(4,128)} %param.12) | copy-start | bytes 388
  25.9 6.4 %copy-start.2 = (s32[4,8]{1,0:T(4,128)S(1)}, s32[4,8]{1,0:T(4,128)}, u32[]{:S(2)}) copy-start(s32[4,8]{1,0:T(4,128)} %param.13) | copy-start | bytes 388
  25.9 6.6 %copy-start = (f32[4,8,256]{2,1,0:T(8,128)S(1)}, f32[4,8,256]{2,1,0:T(8,128)}, u32[]{:S(2)}) copy-start(f32[4,8,256]{2,1,0:T(8,128)} %param.11) | copy-start | bytes 98308
  25.9 47.6 %all-to-all-start.1 = ((f32[96,32,128]{2,1,0:T(8,128)}), f32[96,32,128]{2,1,0:T(8,128)S(1)}, u32[]{:S(2)}, u32[]{:S(2)}) async-start(f32[96,32,128]{2,1,0:T(8,128)} %scatter_fusion), calls=%async_computation.1 | async-start | bytes 3145728 | tf_op jit(solution)/shard_map/all_to_all | solution.py:141
  32.5 30.7 %collective-permute-start = (f32[32,384]{1,0:T(8,128)S(1)}, f32[32,384]{1,0:T(8,128)S(1)}, u32[]{:S(2)}, u32[]{:S(2)}) collective-permute-start(f32[32,384]{1,0:T(8,128)S(1)} %pad_maximum_fusion.2), channel_id=1, source_target_pairs={{0,2},{2,4},{4,6},{6,8},{8,10},{10,12},{12,14},{14,0},{1,3},{3,5},... | collective-permute-start | bytes 147464 | tf_op jit(solution)/shard_map/ppermute | solution.py:149
  34.6 28.7 %collective-permute-start.1 = (f32[32,384]{1,0:T(8,128)S(1)}, f32[32,384]{1,0:T(8,128)S(1)}, u32[]{:S(2)}, u32[]{:S(2)}) collective-permute-start(f32[32,384]{1,0:T(8,128)S(1)} %pad_maximum_fusion.2), channel_id=1, source_target_pairs={{0,4},{2,6},{4,8},{6,10},{8,12},{10,14},{12,0},{14,2},{1,5},{3,7},... | collective-permute-start | bytes 147464 | tf_op jit(solution)/shard_map/ppermute | solution.py:149
  36.0 36.7 %collective-permute-start.2 = (f32[32,384]{1,0:T(8,128)S(1)}, f32[32,384]{1,0:T(8,128)S(1)}, u32[]{:S(2)}, u32[]{:S(2)}) collective-permute-start(f32[32,384]{1,0:T(8,128)S(1)} %pad_maximum_fusion.2), channel_id=1, source_target_pairs={{0,6},{2,8},{4,10},{6,12},{8,14},{10,0},{12,2},{14,4},{1,7},{3,9},... | collective-permute-start | bytes 147464 | tf_op jit(solution)/shard_map/ppermute | solution.py:149
  91.6 1.4 %collective-permute-start.3 = (f32[16,14,128]{2,1,0:T(8,128)S(1)}, f32[16,14,128]{2,1,0:T(8,128)S(1)}, u32[]{:S(2)}, u32[]{:S(2)}) collective-permute-start(f32[16,14,128]{2,1,0:T(8,128)S(1)} %constant_dynamic-slice_fusion), channel_id=1, source_target_pairs={{0,1},{1,0},{2,3},{3,2},{4,5},{5,4},{6,7},{7,6},{8,9},{9,8},{10,11... | collective-permute-start | bytes 344072 | tf_op jit(solution)/shard_map/ppermute | solution.py:187

commit v2 on v1

v2 whole, which is shorter than its diff:
```python
import functools
import math

import jax
import jax.numpy as jnp
from jax import lax
from jax.experimental import pallas as pl
from jax.experimental.pallas import tpu as pltpu
from jax.sharding import PartitionSpec as P

MAXOFF = 256
STOPS = 4
FLOOR_SHARE = 0.25
TEMPLATE_EPS = 1e-06
LANES = 128


def flat_shift(x, by):
    rows = x.shape[-2]
    if by == LANES:
        return pltpu.roll(x, rows - 1, x.ndim - 2)
    lane = lax.broadcasted_iota(jnp.int32, x.shape, x.ndim - 1)
    moved = pltpu.roll(x, LANES - by, x.ndim - 1)
    below = pltpu.roll(moved, rows - 1, x.ndim - 2)
    return jnp.where(lane < LANES - by, moved, below)


def window_total(x, taps):
    span = 1
    while span < taps:
        x = x + flat_shift(x, span)
        span *= 2
    return x


def split(x):
    hi = x.astype(jnp.bfloat16)
    lo = (x - hi.astype(jnp.float32)).astype(jnp.bfloat16)
    return hi, lo


def neighbour(axis, by):
    return lax.rem(lax.axis_index(axis) + by, lax.axis_size(axis))


def stack_kernel(
    gain, half_taps, capacity, src_slot, rows_ref, ids_ref, tmpl_ref, out_ref,
    send_buf, recv_buf, visit_buf, unit_ref, table_ref, win_ref, scale_ref, map_ref, map_smem, part_ref, other_ref,
    send_sem, recv_sem, tsend_sem, trecv_sem, csend_sem, crecv_sem, map_sem,
):
    peers = lax.axis_size("tm")
    me, half = lax.axis_index("tm"), lax.axis_index("chan")
    taps = unit_ref.shape[1]
    pair_rows = unit_ref.shape[0] // STOPS
    blocks = scale_ref.shape[1]
    share = out_ref.shape[1]

    barrier = pltpu.get_barrier_semaphore()

    def greet(k, carry):
        pl.semaphore_signal(
            barrier, inc=1, device_id={"tm": neighbour("tm", k)}, device_id_type=pl.DeviceIdType.MESH
        )
        return carry

    lax.fori_loop(1, peers, greet, 0)
    pl.semaphore_signal(barrier, inc=1, device_id={"chan": 1 - half}, device_id_type=pl.DeviceIdType.MESH)
    pl.semaphore_wait(barrier, peers)

    def visit_copy(by):
        return pltpu.make_async_remote_copy(
            src_ref=visit_buf.at[0],
            dst_ref=visit_buf.at[by],
            send_sem=tsend_sem.at[by],
            recv_sem=trecv_sem.at[by],
            device_id={"tm": neighbour("tm", by)},
            device_id_type=pl.DeviceIdType.MESH,
        )

    def rows_copy(k):
        return pltpu.make_async_remote_copy(
            src_ref=send_buf.at[k],
            dst_ref=recv_buf.at[k],
            send_sem=send_sem.at[k],
            recv_sem=recv_sem.at[k],
            device_id={"tm": neighbour("tm", k)},
            device_id_type=pl.DeviceIdType.MESH,
        )

    def pack(k, buf):
        dest = neighbour("tm", k)
        for r in range(capacity):
            buf[k, r * blocks:(r + 1) * blocks, :] = rows_ref[src_slot[dest * capacity + r]]
        buf[k, capacity * blocks:, :] = ids_ref[dest]

    visit_buf[0] = tmpl_ref[...]
    for by in range(1, STOPS):
        visit_copy(by).start()

    def send_block(k, carry):
        pack(k, send_buf)
        rows_copy(k).start()
        return carry

    lax.fori_loop(1, peers, send_block, 0)
    pack(0, recv_buf)

    u_pos = lax.broadcasted_iota(jnp.int32, (LANES, LANES), 0)
    r_pos = lax.broadcasted_iota(jnp.int32, (LANES, LANES), 1)
    lower = u_pos >= r_pos

    def put_table(pair, which, piece):
        around, full = piece[:, :LANES], piece[:, LANES:]
        zero = jnp.zeros_like(around)
        table_ref[pair, which, :LANES, :LANES] = jnp.where(lower, around, zero).astype(jnp.bfloat16)
        table_ref[pair, which, :LANES, LANES:] = zero.astype(jnp.bfloat16)
        table_ref[pair, which, LANES:, :LANES] = full.astype(jnp.bfloat16)
        table_ref[pair, which, LANES:, LANES:] = jnp.where(lower, zero, around).astype(jnp.bfloat16)

    def put_pair(pair):
        row = jnp.broadcast_to(unit_ref[pl.ds(pair, 1), :], (LANES, taps))
        table = pltpu.roll(row, 0, 1, stride=1, stride_axis=0)
        hi = table.astype(jnp.bfloat16).astype(jnp.float32)
        put_table(pair, 0, hi)
        put_table(pair, 1, table - hi)

    for by in range(STOPS):
        if by > 0:
            visit_copy(by).wait_recv()
        raw = visit_buf[by, :pair_rows, :]
        centred = raw - jnp.mean(raw, axis=-1, keepdims=True)
        energy = jnp.sum(centred * centred, axis=-1, keepdims=True)
        unit_ref[by * pair_rows:(by + 1) * pair_rows, :] = centred / jnp.sqrt(energy + taps * TEMPLATE_EPS)

        def pair_group(group, carry, by=by):
            for j in range(2):
                put_pair(by * pair_rows + group * 2 + j)
            return carry

        lax.fori_loop(0, pair_rows // 2, pair_group, 0)

    unroll = 4 if capacity % 4 == 0 else 1

    def one_row(k, r):
        x = recv_buf[k, pl.ds(pl.multiple_of(r * blocks, 8), blocks), :]
        win_sum = window_total(x, taps)
        win_sq = window_total(x * x, taps)
        variance = win_sq - win_sum * win_sum / taps
        slot = k * capacity + r
        scale_ref[slot] = gain / jnp.sqrt(jnp.maximum(variance, FLOOR_SHARE * taps))
        hi, lo = split(jnp.concatenate([x, pltpu.roll(x, blocks - 1, 0)], axis=1))
        win_ref[slot, :blocks] = hi
        win_ref[slot, blocks:] = lo

    def rows_of(k):
        def group_of(group, carry):
            for j in range(unroll):
                one_row(k, group * unroll + j)
            return carry

        lax.fori_loop(0, capacity // unroll, group_of, 0)

    def arrive(k, carry):
        rows_copy(k).wait_recv()
        rows_of(k)
        return carry

    rows_of(0)
    lax.fori_loop(1, peers, arrive, 0)

    id_rows = recv_buf.shape[1] - capacity * blocks
    order = lax.broadcasted_iota(jnp.int32, (id_rows, LANES), 0)
    for by in range(STOPS):
        wanted = visit_buf[by, pair_rows:pair_rows + 1, :LANES]

        def find(k, found, wanted=wanted):
            held = recv_buf[k, capacity * blocks:, :]
            number = (order + k * capacity).astype(jnp.float32)
            return jnp.maximum(found, jnp.max(jnp.where(held == wanted, number, 0.0), axis=0, keepdims=True))

        found = lax.fori_loop(0, peers, find, jnp.zeros((1, LANES), jnp.float32))
        map_ref[by:by + 1, :] = jnp.clip(found.astype(jnp.int32), 0, peers * capacity - 1)
        map_ref[STOPS + by:STOPS + by + 1, :] = visit_buf[by, pair_rows + 1:pair_rows + 2, :LANES].astype(jnp.int32)
    map_copy = pltpu.make_async_copy(map_ref, map_smem, map_sem)
    map_copy.start()
    map_copy.wait()

    lane = lax.broadcasted_iota(jnp.int32, (blocks, LANES), 1)

    def one_pair(by, place):
        pair = by * pair_rows + place
        slot = jnp.clip(map_smem[by, place], 0, peers * capacity - 1)
        offset = map_smem[STOPS + by, place]
        windows = win_ref[slot]
        first = jnp.dot(windows, table_ref[pair, 0], preferred_element_type=jnp.float32)
        second = jnp.dot(windows[:blocks], table_ref[pair, 1], preferred_element_type=jnp.float32)
        both = first[:blocks] + first[blocks:] + second
        corr = both[:, :LANES] + pltpu.roll(both[:, LANES:], blocks - 1, 0)
        ratio = corr * scale_ref[slot]
        far = offset >= LANES
        low = jnp.where(far, offset - LANES, offset)
        moved = pltpu.roll(ratio, jnp.where(low == 0, 0, LANES - low), 1)
        below = pltpu.roll(moved, blocks - 1, 0)
        below2 = pltpu.roll(moved, blocks - 2, 0)
        return jnp.where(lane < LANES - low, jnp.where(far, below, moved), jnp.where(far, below2, below))

    for by in range(STOPS):
        def one_template(template, carry, by=by):
            total = one_pair(by, template * half_taps)
            for i in range(1, half_taps):
                total = total + one_pair(by, template * half_taps + i)
            place = by * (pair_rows // half_taps) + template
            part_ref[0, place] = total[:share]
            part_ref[1, place] = total[share:2 * share]
            return carry

        lax.fori_loop(0, pair_rows // half_taps, one_template, 0)

    swap = pltpu.make_async_remote_copy(
        src_ref=part_ref.at[1 - half],
        dst_ref=other_ref,
        send_sem=csend_sem,
        recv_sem=crecv_sem,
        device_id={"chan": 1 - half},
        device_id_type=pl.DeviceIdType.MESH,
    )
    swap.start()
    for by in range(1, STOPS):
        visit_copy(by).wait_send()

    def sent(k, carry):
        rows_copy(k).wait_send()
        return carry

    lax.fori_loop(1, peers, sent, 0)
    swap.wait()
    out_ref[...] = part_ref[half] + other_ref[...]


def local(records, row_dest, row_chan, row_len, templates, tmpl_chan, tmpl_off):
    slot_count, sample_count = records.shape
    peers = lax.axis_size("tm")
    half_count = lax.axis_size("chan")
    capacity = slot_count // peers
    template_count, half_taps, tap_count = templates.shape
    assert tap_count == 2 * LANES and half_count == 2
    blocks = sample_count // LANES
    lag_count = sample_count - tap_count - MAXOFF
    share = lag_count // LANES // half_count

    positions = lax.broadcasted_iota(jnp.int32, records.shape, 1)
    masked = jnp.where(positions < row_len[:, None], records, jnp.zeros_like(records))
    masked = masked.reshape(slot_count, blocks, LANES)
    slot_ids = jnp.arange(slot_count, dtype=jnp.int32)
    earlier = (row_dest[:, None] == row_dest[None, :]) & (slot_ids[None, :] < slot_ids[:, None])
    rank_within = jnp.sum(earlier.astype(jnp.int32), axis=1)
    target = jnp.where(row_dest >= 0, row_dest * capacity + rank_within, slot_count)
    here = target[None, :] == slot_ids[:, None]
    src_slot = jnp.sum(jnp.where(here, slot_ids[None, :], 0), axis=1)
    ids = jnp.sum(jnp.where(here, row_chan[None, :] + 1, 0), axis=1) - 1
    id_rows = -(-capacity // 8) * 8
    ids = jnp.pad(ids.reshape(peers, capacity), ((0, 0), (0, id_rows - capacity)), constant_values=-1)
    ids = jnp.broadcast_to(ids.astype(jnp.float32)[:, :, None], (peers, id_rows, LANES))

    pair_rows = template_count * half_taps
    taps_back = jnp.roll(templates.reshape(pair_rows, tap_count)[:, ::-1], 1, axis=1)
    extra = jnp.stack([tmpl_chan.reshape(-1), tmpl_off.reshape(-1)]).astype(jnp.float32)
    extra = jnp.pad(extra, ((0, 6), (0, tap_count - pair_rows)))
    block = jnp.concatenate([taps_back, extra], axis=0)

    pair_count = STOPS * pair_rows
    gain = math.sqrt(tap_count * half_taps * half_count) / (half_taps * half_count)
    smem = pl.BlockSpec(memory_space=pltpu.SMEM)
    vmem = pl.BlockSpec(memory_space=pltpu.VMEM)
    block_rows = capacity * blocks + id_rows
    out = pl.pallas_call(
        functools.partial(stack_kernel, gain, half_taps, capacity),
        out_shape=jax.ShapeDtypeStruct((STOPS * template_count, share, LANES), jnp.float32),
        in_specs=[smem, vmem, vmem, vmem],
        out_specs=vmem,
        scratch_shapes=[
            pltpu.VMEM((peers, block_rows, LANES), jnp.float32),
            pltpu.VMEM((peers, block_rows, LANES), jnp.float32),
            pltpu.VMEM((STOPS,) + block.shape, jnp.float32),
            pltpu.VMEM((pair_count, tap_count), jnp.float32),
            pltpu.VMEM((pair_count, 2, tap_count, tap_count), jnp.bfloat16),
            pltpu.VMEM((slot_count, 2 * blocks, tap_count), jnp.bfloat16),
            pltpu.VMEM((slot_count, blocks, LANES), jnp.float32),
            pltpu.VMEM((2 * STOPS, LANES), jnp.int32),
            pltpu.SMEM((2 * STOPS, LANES), jnp.int32),
            pltpu.VMEM((2, STOPS * template_count, share, LANES), jnp.float32),
            pltpu.VMEM((STOPS * template_count, share, LANES), jnp.float32),
            pltpu.SemaphoreType.DMA((peers,)),
            pltpu.SemaphoreType.DMA((peers,)),
            pltpu.SemaphoreType.DMA((STOPS,)),
            pltpu.SemaphoreType.DMA((STOPS,)),
            pltpu.SemaphoreType.DMA,
            pltpu.SemaphoreType.DMA,
            pltpu.SemaphoreType.DMA,
        ],
        compiler_params=pltpu.CompilerParams(
            vmem_limit_bytes=56 * 2**20, collective_id=0, has_side_effects=True
        ),
        cost_estimate=pl.CostEstimate(
            flops=2 * 3 * pair_count * blocks * tap_count * tap_count,
            bytes_accessed=8 * slot_count * sample_count,
            transcendentals=0,
        ),
    )(src_slot, masked, ids, block)
    return out.reshape(1, STOPS, template_count, share * LANES)


def solution(mesh):
    in_specs = (
        P(("fam", "tm", "chan"), None),
        P(("fam", "tm", "chan")),
        P(("fam", "tm", "chan")),
        P(("fam", "tm", "chan")),
        P(("fam", "tm"), "chan", None),
        P(("fam", "tm"), "chan"),
        P(("fam", "tm"), "chan"),
    )
    out_specs = P(("fam", "tm"), None, None, "chan")
    return jax.shard_map(local, mesh=mesh, in_specs=in_specs, out_specs=out_specs, check_vma=False)
```

time: 95.1 us -> 71.4 us (0.75)
  the two profiles are of different devices: /device:TPU:0 before, /device:TPU:31 now
where the time goes in v2:
time: 71.4 us; the launch traced here: 71.2 us
  Pallas kernels  62.3 us (87%)
  other arithmetic  4.52 us (6%)
  local copies, waits for them, and re-layouts  4.3 us (6%)
    pallas_call x1, Pallas kernels, local(): pl.pallas_call(functools.partial(stack_kernel, gain, half_taps, capacity)...  62.3 us
    unnamed x9, local copies, waits for them, and re-layouts  1.67 us
    unnamed x1, other arithmetic  1.6 us
    reshape x1, local copies, waits for them, and re-layouts, local(): return out.reshape(1, STOPS, template_count, share * LANES)  1.59 us

profile of v2, /device:TPU:31, one launch (start us, length us, event | category | flops | bytes accessed | tf_op | source)
XLA Modules:
  0.0 71.2 jit_solution(384251051966338087)
XLA Ops:
  0.0 0.9 %convert_reduce_fusion = s32[96]{0:T(128)S(1)} fusion(s32[96]{0:T(128)} %param.8), kind=kLoop, calls=%fused_computation.5 | loop fusion | flops 45984 | bytes 768 | tf_op jit(solution)/shard_map/reduce_sum | solution.py:256
  0.9 0.7 compare_select_fusion
  1.6 0.6 select_reduce_fusion
  2.2 1.6 %select_bitcast_fusion = f32[12,8,32,128]{3,1,2,0:T(8,128)S(1)} fusion(f32[96,4096]{1,0:T(8,128)} %param.7, s32[96]{0:T(128)} %param.10), kind=kLoop, calls=%fused_computation | loop fusion | flops 786432 | bytes 3146112
  3.8 0.0 copy-start.1
  3.8 0.0 copy-start.2
  3.8 0.0 copy-start
  3.8 1.4 %copy.8 = f32[12,8,32,128]{3,2,1,0:T(8,128)} copy(f32[12,8,32,128]{3,1,2,0:T(8,128)S(1)} %select_bitcast_fusion) | data formatting | bytes 3145728
  5.3 0.1 sub.7
  5.4 0.7 %broadcast_in_dim.42.ids_ref = f32[8,16,128]{2,1,0:T(8,128)} broadcast(f32[8,16]{1,0:T(8,128)S(1)} %pad_convert_fusion), dimensions={0,1} | broadcast | bytes 66048 | tf_op jit(solution)/shard_map/broadcast_in_dim | solution.py:263
  6.1 0.0 copy-done.1
  6.1 0.1 stack_reshape.7
  6.2 0.0 copy-done.2
  6.2 0.1 stack_reshape.6
  6.3 0.0 copy-done
  6.3 0.1 slice.16
  6.4 0.1 reverse.2
  6.5 0.1 slice.17
  6.6 0.7 select_maximum_fusion.tmpl_ref
  7.3 62.3 %shard_map.73 = f32[16,14,128]{2,1,0:T(8,128)} custom-call(s32[96]{0:T(128)} %get-tuple-element.6.src_slot, f32[96,32,128]{2,1,0:T(8,128)} %bitcast.5, f32[8,16,128]{2,1,0:T(8,128)} %broadcast_in_dim.42.ids_ref, f32[40,256]{1,0:T(8,128)} %select_maximum_fusion.tmpl_ref), custom_call_target="tpu_custom_call" | custom-call | flops 1610612736 | bytes 3145728 | tf_op jit(solution)/shard_map/pallas_call | solution.py:276
  69.6 1.6 %reshape.22 = f32[1,4,4,1792]{3,2,1,0:T(4,128)} reshape(f32[16,14,128]{2,1,0:T(8,128)} %shard_map.73) | data formatting | bytes 229376 | tf_op jit(solution)/shard_map/reshape | solution.py:310
  (4 shorter events, 0.0 us)
Async XLA Ops:
  3.8 2.3 %copy-start.1 = (s32[4,8]{1,0:T(4,128)S(1)}, s32[4,8]{1,0:T(4,128)}, u32[]{:S(2)}) copy-start(s32[4,8]{1,0:T(4,128)} %param.13) | copy-start | bytes 388
  3.8 2.4 %copy-start.2 = (s32[4,8]{1,0:T(4,128)S(1)}, s32[4,8]{1,0:T(4,128)}, u32[]{:S(2)}) copy-start(s32[4,8]{1,0:T(4,128)} %param.12) | copy-start | bytes 388
  3.8 2.4 %copy-start = (f32[4,8,256]{2,1,0:T(8,128)S(1)}, f32[4,8,256]{2,1,0:T(8,128)}, u32[]{:S(2)}) copy-start(f32[4,8,256]{2,1,0:T(8,128)} %param.11) | copy-start | bytes 98308

commit v3 on v2

--- a/solution.py
+++ b/solution.py
@@ -44,8 +44,8 @@
 
 
 def stack_kernel(
-    gain, half_taps, capacity, src_slot, rows_ref, ids_ref, tmpl_ref, out_ref,
-    send_buf, recv_buf, visit_buf, unit_ref, table_ref, win_ref, scale_ref, map_ref, map_smem, part_ref, other_ref,
+    gain, half_taps, capacity, src_slot, row_len, records_ref, ids_ref, tmpl_ref, out_ref,
+    spread_ref, rows_ref, id_ref, send_buf, recv_buf, visit_buf, unit_ref, table_ref, win_ref, scale_ref, map_ref, map_smem, part_ref, other_ref,
     send_sem, recv_sem, tsend_sem, trecv_sem, csend_sem, crecv_sem, map_sem,
 ):
     peers = lax.axis_size("tm")
@@ -53,7 +53,14 @@
     taps = unit_ref.shape[1]
     pair_rows = unit_ref.shape[0] // STOPS
     blocks = scale_ref.shape[1]
-    share = out_ref.shape[1]
+    share = other_ref.shape[1]
+    position = LANES * lax.broadcasted_iota(jnp.int32, (blocks, LANES), 0) + lax.broadcasted_iota(
+        jnp.int32, (blocks, LANES), 1
+    )
+
+    def by_distance(j):
+        step = (j + 1) // 2
+        return peers // 2 + step * (1 - 2 * lax.rem(j, 2))
 
     barrier = pltpu.get_barrier_semaphore()
 
@@ -65,6 +72,16 @@
 
     lax.fori_loop(1, peers, greet, 0)
     pl.semaphore_signal(barrier, inc=1, device_id={"chan": 1 - half}, device_id_type=pl.DeviceIdType.MESH)
+
+    def spread(group, carry):
+        rows = records_ref[pl.ds(pl.multiple_of(group * 8, 8), 8), :]
+        for b in range(blocks):
+            spread_ref[pl.ds(b, 8, stride=blocks), :] = rows[:, b * LANES:(b + 1) * LANES]
+        for r in range(8):
+            rows_ref[group * 8 + r] = spread_ref[r * blocks:(r + 1) * blocks, :]
+        return carry
+
+    lax.fori_loop(0, records_ref.shape[0] // 8, spread, 0)
     pl.semaphore_wait(barrier, peers)
 
     def visit_copy(by):
@@ -90,19 +107,21 @@
     def pack(k, buf):
         dest = neighbour("tm", k)
         for r in range(capacity):
-            buf[k, r * blocks:(r + 1) * blocks, :] = rows_ref[src_slot[dest * capacity + r]]
+            src = src_slot[dest * capacity + r]
+            buf[k, r * blocks:(r + 1) * blocks, :] = jnp.where(position < row_len[src], rows_ref[src], 0.0)
         buf[k, capacity * blocks:, :] = ids_ref[dest]
 
     visit_buf[0] = tmpl_ref[...]
     for by in range(1, STOPS):
         visit_copy(by).start()
 
-    def send_block(k, carry):
+    def send_block(j, carry):
+        k = by_distance(j)
         pack(k, send_buf)
         rows_copy(k).start()
         return carry
 
-    lax.fori_loop(1, peers, send_block, 0)
+    lax.fori_loop(0, peers - 1, send_block, 0)
     pack(0, recv_buf)
 
     u_pos = lax.broadcasted_iota(jnp.int32, (LANES, LANES), 0)
@@ -159,22 +178,25 @@
             return carry
 
         lax.fori_loop(0, capacity // unroll, group_of, 0)
-
-    def arrive(k, carry):
+        id_row = recv_buf[k, capacity * blocks:capacity * blocks + 1, :]
+        id_ref[k] = jnp.transpose(jnp.broadcast_to(id_row, (LANES, LANES)))[:id_ref.shape[1]]
+
+    def arrive(j, carry):
+        k = by_distance(peers - 2 - j)
         rows_copy(k).wait_recv()
         rows_of(k)
         return carry
 
     rows_of(0)
-    lax.fori_loop(1, peers, arrive, 0)
-
-    id_rows = recv_buf.shape[1] - capacity * blocks
+    lax.fori_loop(0, peers - 1, arrive, 0)
+
+    id_rows = id_ref.shape[1]
     order = lax.broadcasted_iota(jnp.int32, (id_rows, LANES), 0)
     for by in range(STOPS):
         wanted = visit_buf[by, pair_rows:pair_rows + 1, :LANES]
 
         def find(k, found, wanted=wanted):
-            held = recv_buf[k, capacity * blocks:, :]
+            held = id_ref[k]
             number = (order + k * capacity).astype(jnp.float32)
             return jnp.maximum(found, jnp.max(jnp.where(held == wanted, number, 0.0), axis=0, keepdims=True))
 
@@ -204,27 +226,32 @@
         below2 = pltpu.roll(moved, blocks - 2, 0)
         return jnp.where(lane < LANES - low, jnp.where(far, below, moved), jnp.where(far, below2, below))
 
+    group_size = pair_rows // half_taps
+
+    def swap(by):
+        group = pl.ds(by * group_size, group_size)
+        return pltpu.make_async_remote_copy(
+            src_ref=part_ref.at[1 - half, group],
+            dst_ref=other_ref.at[group],
+            send_sem=csend_sem.at[by],
+            recv_sem=crecv_sem.at[by],
+            device_id={"chan": 1 - half},
+            device_id_type=pl.DeviceIdType.MESH,
+        )
+
     for by in range(STOPS):
         def one_template(template, carry, by=by):
             total = one_pair(by, template * half_taps)
             for i in range(1, half_taps):
                 total = total + one_pair(by, template * half_taps + i)
-            place = by * (pair_rows // half_taps) + template
+            place = by * group_size + template
             part_ref[0, place] = total[:share]
             part_ref[1, place] = total[share:2 * share]
             return carry
 
-        lax.fori_loop(0, pair_rows // half_taps, one_template, 0)
-
-    swap = pltpu.make_async_remote_copy(
-        src_ref=part_ref.at[1 - half],
-        dst_ref=other_ref,
-        send_sem=csend_sem,
-        recv_sem=crecv_sem,
-        device_id={"chan": 1 - half},
-        device_id_type=pl.DeviceIdType.MESH,
-    )
-    swap.start()
+        lax.fori_loop(0, group_size, one_template, 0)
+        swap(by).start()
+
     for by in range(1, STOPS):
         visit_copy(by).wait_send()
 
@@ -233,8 +260,12 @@
         return carry
 
     lax.fori_loop(1, peers, sent, 0)
-    swap.wait()
-    out_ref[...] = part_ref[half] + other_ref[...]
+    for by in range(STOPS):
+        swap(by).wait()
+        group = pl.ds(by * group_size, group_size)
+        stacks = part_ref[half, group] + other_ref[group]
+        for b in range(share):
+            out_ref[0, by, :, b * LANES:(b + 1) * LANES] = stacks[:, b, :]
 
 
 def local(records, row_dest, row_chan, row_len, templates, tmpl_chan, tmpl_off):
@@ -248,9 +279,6 @@
     lag_count = sample_count - tap_count - MAXOFF
     share = lag_count // LANES // half_count
 
-    positions = lax.broadcasted_iota(jnp.int32, records.shape, 1)
-    masked = jnp.where(positions < row_len[:, None], records, jnp.zeros_like(records))
-    masked = masked.reshape(slot_count, blocks, LANES)
     slot_ids = jnp.arange(slot_count, dtype=jnp.int32)
     earlier = (row_dest[:, None] == row_dest[None, :]) & (slot_ids[None, :] < slot_ids[:, None])
     rank_within = jnp.sum(earlier.astype(jnp.int32), axis=1)
@@ -259,8 +287,8 @@
     src_slot = jnp.sum(jnp.where(here, slot_ids[None, :], 0), axis=1)
     ids = jnp.sum(jnp.where(here, row_chan[None, :] + 1, 0), axis=1) - 1
     id_rows = -(-capacity // 8) * 8
-    ids = jnp.pad(ids.reshape(peers, capacity), ((0, 0), (0, id_rows - capacity)), constant_values=-1)
-    ids = jnp.broadcast_to(ids.astype(jnp.float32)[:, :, None], (peers, id_rows, LANES))
+    ids = jnp.pad(ids.reshape(peers, capacity), ((0, 0), (0, LANES - capacity)), constant_values=-1)
+    ids = jnp.broadcast_to(ids.astype(jnp.float32)[:, None, :], (peers, 8, LANES))
 
     pair_rows = template_count * half_taps
     taps_back = jnp.roll(templates.reshape(pair_rows, tap_count)[:, ::-1], 1, axis=1)
@@ -272,13 +300,16 @@
     gain = math.sqrt(tap_count * half_taps * half_count) / (half_taps * half_count)
     smem = pl.BlockSpec(memory_space=pltpu.SMEM)
     vmem = pl.BlockSpec(memory_space=pltpu.VMEM)
-    block_rows = capacity * blocks + id_rows
+    block_rows = capacity * blocks + 8
     out = pl.pallas_call(
         functools.partial(stack_kernel, gain, half_taps, capacity),
-        out_shape=jax.ShapeDtypeStruct((STOPS * template_count, share, LANES), jnp.float32),
-        in_specs=[smem, vmem, vmem, vmem],
+        out_shape=jax.ShapeDtypeStruct((1, STOPS, template_count, share * LANES), jnp.float32),
+        in_specs=[smem, smem, vmem, vmem, vmem],
         out_specs=vmem,
         scratch_shapes=[
+            pltpu.VMEM((8 * blocks, LANES), jnp.float32),
+            pltpu.VMEM((slot_count, blocks, LANES), jnp.float32),
+            pltpu.VMEM((peers, id_rows, LANES), jnp.float32),
             pltpu.VMEM((peers, block_rows, LANES), jnp.float32),
             pltpu.VMEM((peers, block_rows, LANES), jnp.float32),
             pltpu.VMEM((STOPS,) + block.shape, jnp.float32),
@@ -294,8 +325,8 @@
             pltpu.SemaphoreType.DMA((peers,)),
             pltpu.SemaphoreType.DMA((STOPS,)),
             pltpu.SemaphoreType.DMA((STOPS,)),
-            pltpu.SemaphoreType.DMA,
-            pltpu.SemaphoreType.DMA,
+            pltpu.SemaphoreType.DMA((STOPS,)),
+            pltpu.SemaphoreType.DMA((STOPS,)),
             pltpu.SemaphoreType.DMA,
         ],
         compiler_params=pltpu.CompilerParams(
@@ -306,8 +337,8 @@
             bytes_accessed=8 * slot_count * sample_count,
             transcendentals=0,
         ),
-    )(src_slot, masked, ids, block)
-    return out.reshape(1, STOPS, template_count, share * LANES)
+    )(src_slot, row_len, records, ids, block)
+    return out
 
 
 def solution(mesh):

time: 71.4 us -> 75.4 us (1.056)
  the two profiles are of different devices: /device:TPU:31 before, /device:TPU:15 now
where the time goes in v3:
time: 75.4 us; the launch traced here: 75 us
  Pallas kernels  66.4 us (88%)
  local copies, waits for them, and re-layouts  5.55 us (7%)
  other arithmetic  3.02 us (4%)
    pallas_call x1, Pallas kernels, local(): pl.pallas_call(functools.partial(stack_kernel, gain, half_taps, capacity)...  66.4 us
    unnamed x3, local copies, waits for them, and re-layouts  1.78 us
    slice x2, local copies, waits for them, and re-layouts, local(): jnp.roll(templates.reshape(pair_rows, tap_count)[:, ::-1], 1, axis=1)  1.55 us
    another operation x2, local copies, waits for them, and re-layouts, local(): jnp.stack([tmpl_chan.reshape(-1), tmpl_off.reshape(-1)]).astype(jnp.float32)  1.53 us

profile of v3, /device:TPU:15, one launch (start us, length us, event | category | flops | bytes accessed | tf_op | source)
XLA Modules:
  0.0 75.0 jit_solution(11071473412783917375)
XLA Ops:
  0.0 0.8 %stack_reshape.6 = s32[1,32]{1,0:T(1,128)S(1)} reshape(s32[4,8]{1,0:T(4,128)} %param.12) | data formatting | bytes 256 | tf_op jit(solution)/shard_map/stack;reshape | solution.py:295
  0.8 0.8 %stack_reshape.7 = s32[1,32]{1,0:T(1,128)S(1)} reshape(s32[4,8]{1,0:T(4,128)} %param.13) | data formatting | bytes 256 | tf_op jit(solution)/shard_map/stack;reshape | solution.py:295
  1.5 0.9 %convert_reduce_fusion = s32[96]{0:T(128)S(1)} fusion(s32[96]{0:T(128)} %param.8), kind=kLoop, calls=%fused_computation.3 | loop fusion | flops 45984 | bytes 768 | tf_op jit(solution)/shard_map/reduce_sum | solution.py:284
  2.5 0.7 compare_select_fusion
  3.1 0.7 select_reduce_fusion
  3.8 0.1 sub.7
  3.9 0.7 slice.15
  4.7 0.6 broadcast_in_dim.37.ids_ref
  5.3 0.8 %slice.16 = f32[32,255]{1,0:T(8,128)S(1)} slice(f32[32,256]{1,0:T(8,128)} %bitcast.4), slice={[0:32], [1:256]} | slice | bytes 65280 | tf_op jit(solution)/shard_map/jit(_roll_static)/slice | solution.py:294
  6.1 0.1 reverse.2
  6.2 0.1 slice.17
  6.3 0.7 select_maximum_fusion.tmpl_ref
  7.0 66.4 %shard_map.73 = f32[1,4,4,1792]{3,2,1,0:T(4,128)} custom-call(s32[96]{0:T(128)} %get-tuple-element.6.src_slot, s32[96]{0:T(128)} %row_len.1, f32[96,4096]{1,0:T(8,128)} %records_ref.1, f32[8,8,128]{2,1,0:T(8,128)} %broadcast_in_dim.37.ids_ref, f32[40,256]{1,0:T(8,128)} %select_maximum_fusion.tmpl_ref), custom_call_target="tpu_custom_call" | custom-call | flops 1610612736 | bytes 3145728 | tf_op jit(solution)/shard_map/pallas_call | solution.py:304
  73.5 1.6 %copy.9 = f32[1,4,4,1792]{3,2,1,0:T(4,128)} copy(f32[1,4,4,1792]{3,2,1,0:T(4,128)} %shard_map.73) | data formatting | bytes 229376
  (3 shorter events, 0.0 us)

commit v4 on v3

--- a/solution.py
+++ b/solution.py
@@ -43,8 +43,19 @@
     return lax.rem(lax.axis_index(axis) + by, lax.axis_size(axis))
 
 
+def partner(k):
+    me, peers = lax.axis_index("tm"), lax.axis_size("tm")
+    if peers & (peers - 1):
+        return lax.rem(peers + k - me, peers)
+    other, bit = 0, 1
+    while bit < peers:
+        other = other + bit * lax.rem(lax.rem(me // bit, 2) + lax.rem(k // bit, 2), 2)
+        bit *= 2
+    return other
+
+
 def stack_kernel(
-    gain, half_taps, capacity, src_slot, row_len, records_ref, ids_ref, tmpl_ref, out_ref,
+    gain, half_taps, capacity, src_slot, row_len, records_ref, ids_ref, tmpl_ref, chan_ref, off_ref, out_ref,
     spread_ref, rows_ref, id_ref, send_buf, recv_buf, visit_buf, unit_ref, table_ref, win_ref, scale_ref, map_ref, map_smem, part_ref, other_ref,
     send_sem, recv_sem, tsend_sem, trecv_sem, csend_sem, crecv_sem, map_sem,
 ):
@@ -58,9 +69,10 @@
         jnp.int32, (blocks, LANES), 1
     )
 
+    group_size = pair_rows // half_taps
+
     def by_distance(j):
-        step = (j + 1) // 2
-        return peers // 2 + step * (1 - 2 * lax.rem(j, 2))
+        return peers - 1 - j
 
     barrier = pltpu.get_barrier_semaphore()
 
@@ -100,18 +112,21 @@
             dst_ref=recv_buf.at[k],
             send_sem=send_sem.at[k],
             recv_sem=recv_sem.at[k],
-            device_id={"tm": neighbour("tm", k)},
+            device_id={"tm": partner(k)},
             device_id_type=pl.DeviceIdType.MESH,
         )
 
     def pack(k, buf):
-        dest = neighbour("tm", k)
+        dest = partner(k)
         for r in range(capacity):
             src = src_slot[dest * capacity + r]
             buf[k, r * blocks:(r + 1) * blocks, :] = jnp.where(position < row_len[src], rows_ref[src], 0.0)
-        buf[k, capacity * blocks:, :] = ids_ref[dest]
-
-    visit_buf[0] = tmpl_ref[...]
+        buf[k, capacity * blocks:, :] = jnp.broadcast_to(ids_ref[pl.ds(dest, 1), :], (8, LANES))
+
+    visit_buf[0, :pair_rows, :] = tmpl_ref[...]
+    visit_buf[0, pair_rows:, :] = jnp.zeros((visit_buf.shape[1] - pair_rows, taps), jnp.float32)
+    visit_buf[0, pair_rows:pair_rows + group_size, :half_taps] = chan_ref[...].astype(jnp.float32)
+    visit_buf[0, pair_rows + group_size:pair_rows + 2 * group_size, :half_taps] = off_ref[...].astype(jnp.float32)
     for by in range(1, STOPS):
         visit_copy(by).start()
 
@@ -143,13 +158,22 @@
         put_table(pair, 0, hi)
         put_table(pair, 1, table - hi)
 
+    back_from = lax.broadcasted_iota(jnp.int32, (taps, taps), 0)
+    back_to = lax.broadcasted_iota(jnp.int32, (taps, taps), 1)
+    reverse = jnp.where(lax.rem(back_from + back_to, taps) == 0, 1.0, 0.0)
+
     for by in range(STOPS):
         if by > 0:
             visit_copy(by).wait_recv()
         raw = visit_buf[by, :pair_rows, :]
         centred = raw - jnp.mean(raw, axis=-1, keepdims=True)
         energy = jnp.sum(centred * centred, axis=-1, keepdims=True)
-        unit_ref[by * pair_rows:(by + 1) * pair_rows, :] = centred / jnp.sqrt(energy + taps * TEMPLATE_EPS)
+        unit_ref[by * pair_rows:(by + 1) * pair_rows, :] = jnp.dot(
+            centred / jnp.sqrt(energy + taps * TEMPLATE_EPS),
+            reverse,
+            precision=lax.Precision.HIGHEST,
+            preferred_element_type=jnp.float32,
+        )
 
         def pair_group(group, carry, by=by):
             for j in range(2):
@@ -192,27 +216,30 @@
 
     id_rows = id_ref.shape[1]
     order = lax.broadcasted_iota(jnp.int32, (id_rows, LANES), 0)
-    for by in range(STOPS):
-        wanted = visit_buf[by, pair_rows:pair_rows + 1, :LANES]
+    visit_count = STOPS * group_size
+    for row in range(visit_count):
+        by, template = divmod(row, group_size)
+        at = pair_rows + template
+        wanted = visit_buf[by, at:at + 1, :LANES]
 
         def find(k, found, wanted=wanted):
-            held = id_ref[k]
             number = (order + k * capacity).astype(jnp.float32)
-            return jnp.maximum(found, jnp.max(jnp.where(held == wanted, number, 0.0), axis=0, keepdims=True))
-
-        found = lax.fori_loop(0, peers, find, jnp.zeros((1, LANES), jnp.float32))
-        map_ref[by:by + 1, :] = jnp.clip(found.astype(jnp.int32), 0, peers * capacity - 1)
-        map_ref[STOPS + by:STOPS + by + 1, :] = visit_buf[by, pair_rows + 1:pair_rows + 2, :LANES].astype(jnp.int32)
+            return jnp.maximum(found, jnp.max(jnp.where(id_ref[k] == wanted, number, 0.0), axis=0, keepdims=True))
+
+        found = lax.fori_loop(0, peers, find, jnp.zeros((1, LANES), jnp.float32), unroll=min(peers, 8))
+        map_ref[row:row + 1, :] = jnp.clip(found.astype(jnp.int32), 0, peers * capacity - 1)
+        at = at + group_size
+        map_ref[visit_count + row:visit_count + row + 1, :] = visit_buf[by, at:at + 1, :LANES].astype(jnp.int32)
     map_copy = pltpu.make_async_copy(map_ref, map_smem, map_sem)
     map_copy.start()
     map_copy.wait()
 
     lane = lax.broadcasted_iota(jnp.int32, (blocks, LANES), 1)
 
-    def one_pair(by, place):
-        pair = by * pair_rows + place
-        slot = jnp.clip(map_smem[by, place], 0, peers * capacity - 1)
-        offset = map_smem[STOPS + by, place]
+    def one_pair(row, i):
+        pair = row * half_taps + i
+        slot = jnp.clip(map_smem[row, i], 0, peers * capacity - 1)
+        offset = map_smem[visit_count + row, i]
         windows = win_ref[slot]
         first = jnp.dot(windows, table_ref[pair, 0], preferred_element_type=jnp.float32)
         second = jnp.dot(windows[:blocks], table_ref[pair, 1], preferred_element_type=jnp.float32)
@@ -226,8 +253,6 @@
         below2 = pltpu.roll(moved, blocks - 2, 0)
         return jnp.where(lane < LANES - low, jnp.where(far, below, moved), jnp.where(far, below2, below))
 
-    group_size = pair_rows // half_taps
-
     def swap(by):
         group = pl.ds(by * group_size, group_size)
         return pltpu.make_async_remote_copy(
@@ -241,10 +266,10 @@
 
     for by in range(STOPS):
         def one_template(template, carry, by=by):
-            total = one_pair(by, template * half_taps)
+            place = by * group_size + template
+            total = one_pair(place, 0)
             for i in range(1, half_taps):
-                total = total + one_pair(by, template * half_taps + i)
-            place = by * group_size + template
+                total = total + one_pair(place, i)
             part_ref[0, place] = total[:share]
             part_ref[1, place] = total[share:2 * share]
             return carry
@@ -288,14 +313,10 @@
     ids = jnp.sum(jnp.where(here, row_chan[None, :] + 1, 0), axis=1) - 1
     id_rows = -(-capacity // 8) * 8
     ids = jnp.pad(ids.reshape(peers, capacity), ((0, 0), (0, LANES - capacity)), constant_values=-1)
-    ids = jnp.broadcast_to(ids.astype(jnp.float32)[:, None, :], (peers, 8, LANES))
+    ids = ids.astype(jnp.float32)
 
     pair_rows = template_count * half_taps
-    taps_back = jnp.roll(templates.reshape(pair_rows, tap_count)[:, ::-1], 1, axis=1)
-    extra = jnp.stack([tmpl_chan.reshape(-1), tmpl_off.reshape(-1)]).astype(jnp.float32)
-    extra = jnp.pad(extra, ((0, 6), (0, tap_count - pair_rows)))
-    block = jnp.concatenate([taps_back, extra], axis=0)
-
+    visit_rows = pair_rows + -(-2 * template_count // 8) * 8
     pair_count = STOPS * pair_rows
     gain = math.sqrt(tap_count * half_taps * half_count) / (half_taps * half_count)
     smem = pl.BlockSpec(memory_space=pltpu.SMEM)
@@ -304,7 +325,7 @@
     out = pl.pallas_call(
         functools.partial(stack_kernel, gain, half_taps, capacity),
         out_shape=jax.ShapeDtypeStruct((1, STOPS, template_count, share * LANES), jnp.float32),
-        in_specs=[smem, smem, vmem, vmem, vmem],
+        in_specs=[smem, smem, vmem, vmem, vmem, vmem, vmem],
         out_specs=vmem,
         scratch_shapes=[
             pltpu.VMEM((8 * blocks, LANES), jnp.float32),
@@ -312,13 +333,13 @@
             pltpu.VMEM((peers, id_rows, LANES), jnp.float32),
             pltpu.VMEM((peers, block_rows, LANES), jnp.float32),
             pltpu.VMEM((peers, block_rows, LANES), jnp.float32),
-            pltpu.VMEM((STOPS,) + block.shape, jnp.float32),
+            pltpu.VMEM((STOPS, visit_rows, tap_count), jnp.float32),
             pltpu.VMEM((pair_count, tap_count), jnp.float32),
             pltpu.VMEM((pair_count, 2, tap_count, tap_count), jnp.bfloat16),
             pltpu.VMEM((slot_count, 2 * blocks, tap_count), jnp.bfloat16),
             pltpu.VMEM((slot_count, blocks, LANES), jnp.float32),
-            pltpu.VMEM((2 * STOPS, LANES), jnp.int32),
-            pltpu.SMEM((2 * STOPS, LANES), jnp.int32),
+            pltpu.VMEM((2 * STOPS * template_count, LANES), jnp.int32),
+            pltpu.SMEM((2 * STOPS * template_count, LANES), jnp.int32),
             pltpu.VMEM((2, STOPS * template_count, share, LANES), jnp.float32),
             pltpu.VMEM((STOPS * template_count, share, LANES), jnp.float32),
             pltpu.SemaphoreType.DMA((peers,)),
@@ -337,7 +358,7 @@
             bytes_accessed=8 * slot_count * sample_count,
             transcendentals=0,
         ),
-    )(src_slot, row_len, records, ids, block)
+    )(src_slot, row_len, records, ids, templates.reshape(pair_rows, tap_count), tmpl_chan, tmpl_off)
     return out
 
 

time: 75.4 us -> 69.5 us (0.922)
  the two profiles are of different devices: /device:TPU:15 before, /device:TPU:0 now
where the time goes in v4:
time: 69.5 us; the launch traced here: 69.3 us
  Pallas kernels  64.7 us (93%)
  other arithmetic  2.91 us (4%)
  local copies, waits for them, and re-layouts  1.63 us (2%)
    pallas_call x1, Pallas kernels, local(): pl.pallas_call(functools.partial(stack_kernel, gain, half_taps, capacity)...  64.7 us
    unnamed x1, local copies, waits for them, and re-layouts  1.55 us

profile of v4, /device:TPU:0, one launch (start us, length us, event | category | flops | bytes accessed | tf_op | source)
XLA Modules:
  0.0 69.3 jit_solution(13013434228160841214)
XLA Ops:
  0.0 0.9 %convert_reduce_fusion = s32[96]{0:T(128)S(1)} fusion(s32[96]{0:T(128)} %param.8), kind=kLoop, calls=%fused_computation.3 | loop fusion | flops 45984 | bytes 768 | tf_op jit(solution)/shard_map/reduce_sum | solution.py:309
  0.9 0.7 compare_select_fusion
  1.6 0.7 %select_reduce_fusion = (s32[96]{0:T(128)S(1)}, s32[96]{0:T(128)}) fusion(s32[96]{0:T(128)S(1)} %get-tuple-element.8, s32[96]{0:T(128)S(1)} %get-tuple-element.7), kind=kLoop, calls=%fused_computation | loop fusion | flops 45888 | bytes 1536 | tf_op jit(solution)/shard_map/reduce_sum | solution.py:313
  2.3 0.1 sub.7
  2.4 0.6 pad_convert_fusion.ids_ref
  3.0 64.7 %shard_map.73 = f32[1,4,4,1792]{3,2,1,0:T(4,128)} custom-call(s32[96]{0:T(128)} %get-tuple-element.6.src_slot, s32[96]{0:T(128)} %row_len.1, f32[96,4096]{1,0:T(8,128)} %records_ref.1, f32[8,128]{1,0:T(8,128)} %pad_convert_fusion.ids_ref, f32[32,256]{1,0:T(8,128)} %bitcast.1, s32[4,8]{1,0:T(4,128)} %chan_ref.1, s32[4,8]{1,0:T(4,128)} %off_ref.1), custom_call_target="tpu_custom_call" | custom-call | flops 1610612736 | bytes 3145728 | tf_op jit(solution)/shard_map/pallas_call | solution.py:325
  67.7 1.6 %copy.9 = f32[1,4,4,1792]{3,2,1,0:T(4,128)} copy(f32[1,4,4,1792]{3,2,1,0:T(4,128)} %shard_map.73) | data formatting | bytes 229376
  (1 shorter events, 0.0 us)

commit v5 on v4

--- a/solution.py
+++ b/solution.py
@@ -45,8 +45,7 @@
 
 def partner(k):
     me, peers = lax.axis_index("tm"), lax.axis_size("tm")
-    if peers & (peers - 1):
-        return lax.rem(peers + k - me, peers)
+    assert peers & (peers - 1) == 0
     other, bit = 0, 1
     while bit < peers:
         other = other + bit * lax.rem(lax.rem(me // bit, 2) + lax.rem(k // bit, 2), 2)
@@ -71,8 +70,8 @@
 
     group_size = pair_rows // half_taps
 
-    def by_distance(j):
-        return peers - 1 - j
+    def turn(j):
+        return half * (peers - 1 - j) + (1 - half) * (j + 1)
 
     barrier = pltpu.get_barrier_semaphore()
 
@@ -131,7 +130,7 @@
         visit_copy(by).start()
 
     def send_block(j, carry):
-        k = by_distance(j)
+        k = turn(j)
         pack(k, send_buf)
         rows_copy(k).start()
         return carry
@@ -206,7 +205,7 @@
         id_ref[k] = jnp.transpose(jnp.broadcast_to(id_row, (LANES, LANES)))[:id_ref.shape[1]]
 
     def arrive(j, carry):
-        k = by_distance(peers - 2 - j)
+        k = turn(j)
         rows_copy(k).wait_recv()
         rows_of(k)
         return carry

time: 69.5 us -> 67.4 us (0.970)
  Pallas kernels: 64.7 us -> 62.7 us
    pallas_call x1, Pallas kernels: 64.7 us -> 62.7 us  [local(): pl.pallas_call(functools.partial(stack_kernel, gain, half_taps, capacity)...]
where the time goes in v5:
time: 67.4 us; the launch traced here: 67.2 us
  Pallas kernels  62.7 us (93%)
  other arithmetic  2.91 us (4%)
  local copies, waits for them, and re-layouts  1.63 us (2%)
    pallas_call x1, Pallas kernels, local(): pl.pallas_call(functools.partial(stack_kernel, gain, half_taps, capacity)...  62.7 us
    unnamed x1, local copies, waits for them, and re-layouts  1.55 us

profile of v5, /device:TPU:0, one launch (start us, length us, event | category | flops | bytes accessed | tf_op | source)
XLA Modules:
  0.0 67.2 jit_solution(9182612784217076041)
XLA Ops:
  0.0 0.9 %convert_reduce_fusion = s32[96]{0:T(128)S(1)} fusion(s32[96]{0:T(128)} %param.8), kind=kLoop, calls=%fused_computation.3 | loop fusion | flops 45984 | bytes 768 | tf_op jit(solution)/shard_map/reduce_sum | solution.py:308
  0.9 0.7 %compare_select_fusion = (s32[96]{0:T(128)S(1)}, s32[96]{0:T(128)S(1)}) fusion(s32[96]{0:T(128)} %param.8, s32[96]{0:T(128)S(1)} %convert_reduce_fusion, s32[96]{0:T(128)} %param.9), kind=kLoop, calls=%fused_computation.7 | loop fusion | flops 480 | bytes 1920 | tf_op jit(solution)/shard_map/jit(_where)/select_n | solution.py:309
  1.6 0.7 %select_reduce_fusion = (s32[96]{0:T(128)S(1)}, s32[96]{0:T(128)}) fusion(s32[96]{0:T(128)S(1)} %get-tuple-element.8, s32[96]{0:T(128)S(1)} %get-tuple-element.7), kind=kLoop, calls=%fused_computation | loop fusion | flops 45888 | bytes 1536 | tf_op jit(solution)/shard_map/reduce_sum | solution.py:312
  2.3 0.1 sub.7
  2.4 0.6 pad_convert_fusion.ids_ref
  3.0 62.7 %shard_map.73 = f32[1,4,4,1792]{3,2,1,0:T(4,128)} custom-call(s32[96]{0:T(128)} %get-tuple-element.6.src_slot, s32[96]{0:T(128)} %row_len.1, f32[96,4096]{1,0:T(8,128)} %records_ref.1, f32[8,128]{1,0:T(8,128)} %pad_convert_fusion.ids_ref, f32[32,256]{1,0:T(8,128)} %bitcast.1, s32[4,8]{1,0:T(4,128)} %chan_ref.1, s32[4,8]{1,0:T(4,128)} %off_ref.1), custom_call_target="tpu_custom_call" | custom-call | flops 1610612736 | bytes 3145728 | tf_op jit(solution)/shard_map/pallas_call | solution.py:324
  65.7 1.6 %copy.9 = f32[1,4,4,1792]{3,2,1,0:T(4,128)} copy(f32[1,4,4,1792]{3,2,1,0:T(4,128)} %shard_map.73) | data formatting | bytes 229376
  (1 shorter events, 0.0 us)
